TPU v7x, 256 devices: a whole 4x4x8 slice. The times are simulated.
256 devices in a mesh: outer: 16 (over y, x), inner: 16 (over z, core).
Axes of the slice: x: 4, y: 4, z: 8, core: 2. Of those that a mesh axis runs over, the one named last changes fastest.
Arguments:
- tokens: bfloat16 [98304, 1024], P(('outer', 'inner')), may hold values from -6 to 6
- log_decay: float32 [98304, 16], P(('outer', 'inner')), may hold values from -1 to 0, as said below
- query_weight: bfloat16 [1024, 1024], replicated, may hold values from -0.1875 to 0.1875
- key_weight: bfloat16 [1024, 1024], replicated, may hold values from -0.1875 to 0.1875
- value_weight: bfloat16 [1024, 1024], replicated, may hold values from -0.1875 to 0.1875
- norm_gain: float32 [1024], replicated, may hold values from 0.1 to 1.9
- output_weight: bfloat16 [1024, 1024], replicated, may hold values from -0.1875 to 0.1875
Outputs:
- mixed: bfloat16 [98304, 1024], P(('outer', 'inner'))
Inputs may be any that keep to these rules, and one draw needn't show every extreme that they name: log_decay is negative.
All inputs are finite; a program needn't handle non-finite values.
Results may differ from a plain program's by a relative error of at most 0.0063.
Values sent between devices are 32-bit elements; how exact they have to be, the bound alone decides.
A program may use at most 320 MiB of HBM per device.

v0:
```python
import jax
import jax.numpy as jnp
from jax import lax
from jax.sharding import PartitionSpec as P


def prefix(value, axis, join, neutral):
    count, mine = (lax.axis_size(axis), lax.axis_index(axis))
    pieces = jax.tree.map(lambda part: lax.all_gather(part, axis), value)
    running = jax.tree.map(
        lambda part, zero: jnp.full_like(part, 0) + jnp.asarray(zero, part.dtype), value, neutral
    )

    def lap(position, running):
        longer = join(running, jax.tree.map(lambda part: part[position], pieces))
        return jax.tree.map(lambda new, old: jnp.where(position < mine, new, old), longer, running)

    return lax.fori_loop(0, count - 1, lap, running)


def broadcast(value, axis, source):
    kept = jnp.where(lax.axis_index(axis) == source, value, 0).astype(value.dtype)
    return lax.psum(kept, axis)


def local_head(q_head, k_head, v_head, g_head):
    cum = jnp.cumsum(g_head)
    count = cum.shape[0]
    rows = lax.broadcasted_iota(jnp.int32, (count, count), 0)
    cols = lax.broadcasted_iota(jnp.int32, (count, count), 1)
    lower = cols <= rows
    diff = jnp.where(lower, cum[:, None] - cum[None, :], 0.0)
    decay = jnp.where(lower, jnp.exp(diff), 0.0)
    scores = jnp.dot(q_head, k_head.T, preferred_element_type=jnp.float32)
    weights = (scores * decay).astype(jnp.bfloat16)
    intra = jnp.dot(weights, v_head, preferred_element_type=jnp.float32)
    last = cum[-1]
    scaled = (k_head.astype(jnp.float32) * jnp.exp(last - cum)[:, None]).astype(jnp.bfloat16)
    local = jnp.dot(scaled.T, v_head, preferred_element_type=jnp.float32)
    return (intra, local, jnp.exp(last))


def combine(earlier, later):
    return (earlier[0] * later[0], later[0][:, None, None] * earlier[1] + later[1])


def shards(tokens, log_decay, query_weight, key_weight, value_weight, norm_gain, output_weight):
    count = tokens.shape[0]
    heads = log_decay.shape[1]
    queries = jax.nn.silu(jnp.dot(tokens, query_weight, preferred_element_type=jnp.float32)).astype(
        jnp.bfloat16
    )
    keys = jax.nn.silu(jnp.dot(tokens, key_weight, preferred_element_type=jnp.float32)).astype(
        jnp.bfloat16
    )
    value_rows = jnp.dot(tokens, value_weight, preferred_element_type=jnp.float32).astype(
        jnp.bfloat16
    )
    split = lambda arr: arr.reshape(count, heads, -1).transpose(1, 0, 2)
    queries, keys, value_rows = (split(queries), split(keys), split(value_rows))
    intra, local, fall = lax.map(
        lambda token_parts: local_head(*token_parts), (queries, keys, value_rows, log_decay.T)
    )
    own = (fall, local)
    identity = (jnp.ones_like(fall), jnp.zeros_like(local))
    inner_before = prefix(own, "inner", combine, identity)
    inclusive = combine(inner_before, own)
    total = (
        broadcast(inclusive[0], "inner", lax.axis_size("inner") - 1),
        broadcast(inclusive[1], "inner", lax.axis_size("inner") - 1),
    )
    outer_before = prefix(total, "outer", combine, identity)
    incoming = combine(outer_before, inner_before)[1]
    cum = jnp.cumsum(log_decay, axis=0)
    qfloat = queries.astype(jnp.float32)
    inter = (
        jnp.einsum("htd,hde->the", qfloat, incoming, precision=lax.Precision.HIGHEST)
        * jnp.exp(cum)[:, :, None]
    )
    attended = intra.transpose(1, 0, 2) + inter
    scale = lax.rsqrt(jnp.mean(attended * attended, axis=-1, keepdims=True) + 1e-05)
    normalized_output = ((attended * scale).reshape(count, -1) * norm_gain).astype(jnp.bfloat16)
    return jnp.dot(normalized_output, output_weight, preferred_element_type=jnp.float32).astype(
        jnp.bfloat16
    )


def solution(mesh):
    in_specs = (P(("outer", "inner"), None), P(("outer", "inner"), None), P(), P(), P(), P(), P())
    out_specs = P(("outer", "inner"), None)
    return jax.shard_map(shards, mesh=mesh, in_specs=in_specs, out_specs=out_specs, check_vma=False)
```

profile of v0, /device:TPU:1, one launch (start us, length us, event | category | flops | bytes accessed | tf_op | source)
XLA Modules:
  0.0 440.0 jit_solution(5234878555848884277)
XLA Ops:
  8.1 3.2 multiply_convert_fusion.2
  12.8 3.9 multiply_convert_fusion.1
  16.6 2.3 copy.24
  18.9 3.7 convolution_convert_fusion.1
  22.6 2.3 copy.25
  25.0 115.7 %while.47 = (s32[]{:T(128)}, f32[16,384,64]{1,2,0:T(8,128)}, f32[16,64,64]{2,1,0:T(8,128)}, f32[16]{0:T(128)S(1)}, bf16[16,384,64]{1,2,0:T(8,128)(2,1)S(1)}, /*i...) while((s32[]{:T(128)}, f32[16,384,64]{1,2,0:T(8,128)}, ...), condition=%wide.region_3.4_spmd.clone, body=%wide.region_0.3_spmd.sunk.clone | while | flops 41902472 | bytes 594653 | solution.py:61
  29.5 1.9 fusion.74
  36.7 1.9 fusion.74
  43.9 1.9 fusion.74
  51.2 1.9 fusion.74
  58.4 1.9 fusion.74
  65.6 1.9 fusion.74
  72.9 1.9 fusion.74
  80.1 1.9 fusion.74
  87.3 1.9 fusion.74
  94.5 1.9 fusion.74
  101.8 1.9 fusion.74
  109.0 1.9 fusion.74
  116.2 1.9 fusion.74
  123.5 1.9 fusion.74
  130.7 1.9 fusion.74
  137.9 1.9 fusion.74
  142.2 28.4 %all-reduce = f32[256]{0:T(256)S(1)} all-reduce(f32[256]{0:T(256)S(1)} %dynamic-update-slice), channel_id=2, replica_groups=mesh['outer'=16,'inner'=16] {'inner'}, use_global_device_ids=true, to_apply=%add | all-reduce | flops 256 | bytes 2048
  170.7 30.5 %all-gather.8.cloned.1.call-done = f32[256,64,64]{2,1,0:T(8,128)} async-done(((f32[16,64,64]{2,1,0:T(8,128)}), f32[256,64,64]{2,1,0:T(8,128)}) %all-gather.8.cloned.1.call-update) | async-done | bytes 4194320 | tf_op jit(solution)/shard_map/all_gather | solution.py:9
  201.2 18.3 %while.48 = (s32[]{:T(128)}, f32[16]{0:T(128)S(1)}, f32[16,64,64]{2,1,0:T(8,128)S(1)}, s32[]{:T(128)}, f32[16,16]{1,0:T(8,128)S(1)}, /*index=5*/f32[16,16,64,64]{3,2,1,0:T(8,128)}) while((s32[]{:T(128)}, f32[16]{0:T(128)S(1)}, f32[16,64,64]{2,1,0:T(8,128)S(1)}, s32[]{:T(128)}, f32[16,16]{1,0:T(8,128)S(1)}, ...), condition=%wide.region_5.6_spmd.clone.clone, body=%wide.region_4.5_spmd.clone.sunk.clone | while | flops 262196 | bytes 786851 | solution.py:18
  219.5 2.0 select_bitcast_fusion
  221.5 107.8 %all-reduce.3.cloned.1.call-done = f32[1,16,64,64]{3,2,1,0:T(8,128)} async-done(((f32[1,16,64,64]{3,2,1,0:T(8,128)}), f32[1,16,64,64]{3,2,1,0:T(8,128)}) %all-reduce.3.cloned.1.call-update) | async-done | bytes 262160 | tf_op jit(solution)/shard_map/psum | solution.py:23
  330.5 23.6 %psum.14 = f32[1,16]{1,0:T(1,128)S(1)} all-reduce(f32[1,16]{1,0:T(1,128)S(1)} %fusion.37), channel_id=1, replica_groups=mesh['outer'=16,'inner'=16] {'inner'}, use_global_device_ids=true, to_apply=%region_6.7 | all-reduce | flops 16 | bytes 128 | tf_op jit(solution)/shard_map/psum | solution.py:23
  354.1 16.7 %all-gather.2 = f32[16,1,16]{2,1,0:T(1,128)S(1)} all-gather(f32[1,1,16]{2,1,0:T(1,128)S(1)} %bitcast.147), channel_id=1, replica_groups=mesh['outer'=16,'inner'=16] {'outer'}, dimensions={0}, use_global_device_ids=true | all-gather | bytes 1088 | tf_op jit(solution)/shard_map/all_gather | solution.py:9
  370.9 37.3 %all-gather.6.cloned.1.call-done = f32[16,16,64,64]{3,2,1,0:T(8,128)} async-done(((f32[1,16,64,64]{3,2,1,0:T(8,128)}), f32[16,16,64,64]{3,2,1,0:T(8,128)}) %all-gather.6.cloned.1.call-update) | async-done | bytes 4194320 | tf_op jit(solution)/shard_map/all_gather | solution.py:9
  408.2 18.2 %while.49 = (s32[]{:T(128)}, f32[16,64,64]{2,1,0:T(8,128)S(1)}, s32[]{:T(128)}, f32[16,16]{1,0:T(8,128)S(1)}, f32[16,16,64,64]{3,2,1,0:T(8,128)}) while((s32[]{:T(128)}, f32[16,64,64]{2,1,0:T(8,128)S(1)}, s32[]{:T(128)}, f32[16,16]{1,0:T(8,128)S(1)}, f32[16,16,64,64]{3,2,1,0:T(8,128)}) %tuple.108), condition=%wide.region_9.10_spmd.clone.clone, body=%wide.region_8.9_spmd.clone.sunk.clone | while | flops 262148 | bytes 786713 | solution.py:18
  426.4 2.9 multiply_reduce_fusion
  (291 shorter events, 118.9 us)
Async XLA Ops:
  6.5 1.6 copy-start
  6.5 194.6 %all-gather.8.cloned.1.call-start = ((), (), s32[]{:S(2)}) async-start(), calls=%async_computation.2 | async-start | bytes 8912896 | tf_op jit(solution)/shard_map/all_gather | solution.py:9
  22.6 2.3 copy-start.3
  25.0 115.8 %copy-start.5 = (u32[256]{0:T(256)S(1)}, u32[256]{0:T(256)}, u32[]{:S(2)}) copy-start(u32[256]{0:T(256)} %constant.98) | copy-start | bytes 3076
  140.6 80.8 %copy-start.1 = (bf16[16,384,64]{1,2,0:T(8,128)(2,1)}, bf16[16,384,64]{1,2,0:T(8,128)(2,1)S(1)}, u32[]{:S(2)}) copy-start(bf16[16,384,64]{1,2,0:T(8,128)(2,1)S(1)} %get-tuple-element.586) | copy-start | bytes 2359300
  140.7 188.6 %all-reduce.3.cloned.1.call-start = ((), (), s32[]{:S(2)}) async-start(), calls=%async_computation | async-start | bytes 1048576 | tf_op jit(solution)/shard_map/psum | solution.py:23
  221.5 186.7 %all-gather.6.cloned.1.call-start = ((), (), s32[]{:S(2)}) async-start(), calls=%async_computation.1 | async-start | bytes 8912896 | tf_op jit(solution)/shard_map/all_gather | solution.py:9
  429.3 0.7 copy-start.4
  430.0 1.6 copy-start.2
Sparse Core Ops, SparseCore 0:
  140.8 60.3 all-gather.7
  221.6 107.6 all-reduce.2
  332.0 76.1 all-gather.5
where the time goes:
time: 445 us; the launch traced here: 440 us
  waiting for transfers between devices  176 us (40%)
  matrix products  73.1 us (16%)
  blocking collectives  68.7 us (15%)
  other arithmetic  55.9 us (13%)
  local copies, waits for them, and re-layouts  40.5 us (9%)
  between operations  13.8 us (3%)
  loops' own time  12.1 us (3%)
    psum x1, waiting for transfers between devices, broadcast(): return lax.psum(kept, axis)  108 us
    all_gather x2, waiting for transfers between devices, prefix(): pieces = jax.tree.map(lambda part: lax.all_gather(part, axis), value)  67.8 us
    select_n x45, other arithmetic, lap(): jnp.where(position < mine, new, old)  35.5 us
    dot_general x16, matrix products, local_head(): intra = jnp.dot(weights, v_head, preferred_element_type=jnp.float32)  30.6 us
    unnamed x1, blocking collectives  28.4 us
    dot_general x16, matrix products, local_head(): local = jnp.dot(scaled.T, v_head, preferred_element_type=jnp.float32)  27 us
    psum x1, blocking collectives, broadcast(): return lax.psum(kept, axis)  23.6 us
    all_gather x1, blocking collectives, prefix(): pieces = jax.tree.map(lambda part: lax.all_gather(part, axis), value)  16.7 us
  transfers between devices with their start and end apart: 3, of which 3 were waited for; matrix products, arithmetic and copies ran while one was open for 0% of the time, Pallas kernels for 0%

commit v1 on v0

--- a/solution.py
+++ b/solution.py
@@ -20,7 +20,7 @@
 
 def broadcast(value, axis, source):
     kept = jnp.where(lax.axis_index(axis) == source, value, 0).astype(value.dtype)
-    return lax.psum(kept, axis)
+    return jnp.sum(lax.all_gather(kept, axis), axis=0)
 
 
 def local_head(q_head, k_head, v_head, g_head):

time: 445 us -> 393 us (0.88)
  waiting for transfers between devices: 176 us -> 99.2 us
  blocking collectives: 68.7 us -> 85.9 us
  other arithmetic: 55.9 us -> 61.3 us
    psum x1 -> x0, waiting for transfers between devices: 108 us -> none  [broadcast(): return lax.psum(kept, axis)]
    unnamed x1 -> x3, blocking collectives: 28.4 us -> 85.9 us
    all_gather x0 -> x1, waiting for transfers between devices: none -> 54.5 us  [broadcast(): return jnp.sum(lax.all_gather(kept, axis), axis=0)]
    psum x1 -> x0, blocking collectives: 23.6 us -> none  [broadcast(): return lax.psum(kept, axis)]
    all_gather x2, waiting for transfers between devices: 67.8 us -> 44.6 us  [prefix(): pieces = jax.tree.map(lambda part: lax.all_gather(part, axis), value)]
    all_gather x1 -> x0, blocking collectives: 16.7 us -> none  [prefix(): pieces = jax.tree.map(lambda part: lax.all_gather(part, axis), value)]
    reduce_sum x0 -> x2, other arithmetic: none -> 5.25 us  [broadcast(): return jnp.sum(lax.all_gather(kept, axis), axis=0)]
  transfers between devices with their start and end apart: 3 -> 3, of which waited for: 3 -> 3; matrix products, arithmetic and copies ran while one was open for 0% -> 1% of each run, Pallas kernels for 0% -> 0%
where the time goes in v1:
time: 393 us; the launch traced here: 388 us
  waiting for transfers between devices  99.2 us (25%)
  blocking collectives  85.9 us (22%)
  matrix products  73.1 us (19%)
  other arithmetic  61.3 us (16%)
  local copies, waits for them, and re-layouts  41.5 us (11%)
  between operations  14.5 us (4%)
  loops' own time  12.1 us (3%)
    unnamed x3, blocking collectives  85.9 us
    all_gather x1, waiting for transfers between devices, broadcast(): return jnp.sum(lax.all_gather(kept, axis), axis=0)  54.5 us
    all_gather x2, waiting for transfers between devices, prefix(): pieces = jax.tree.map(lambda part: lax.all_gather(part, axis), value)  44.6 us
    select_n x45, other arithmetic, lap(): jnp.where(position < mine, new, old)  35.5 us
    dot_general x16, matrix products, local_head(): intra = jnp.dot(weights, v_head, preferred_element_type=jnp.float32)  30.6 us
    dot_general x16, matrix products, local_head(): local = jnp.dot(scaled.T, v_head, preferred_element_type=jnp.float32)  27 us
    dynamic_slice x48, local copies, waits for them, and re-layouts, shards(): lax.map(lambda token_parts: local_head(*token_parts), (queries, keys, val...  15.3 us
    another operation x1, loops' own time, shards(): lax.map(lambda token_parts: local_head(*token_parts), (queries, keys, val...  11.3 us
  transfers between devices with their start and end apart: 3, of which 3 were waited for; matrix products, arithmetic and copies ran while one was open for 1% of the time, Pallas kernels for 0%

profile of v1, /device:TPU:1, one launch (start us, length us, event | category | flops | bytes accessed | tf_op | source)
XLA Modules:
  0.0 387.7 jit_solution(10563191037203842705)
XLA Ops:
  8.1 3.2 multiply_convert_fusion.2
  12.8 3.9 multiply_convert_fusion.1
  16.6 2.3 copy.33
  18.9 3.7 convolution_convert_fusion.1
  22.6 2.3 copy.34
  25.0 115.7 %while.47 = (s32[]{:T(128)}, f32[16,384,64]{1,2,0:T(8,128)}, f32[16,64,64]{2,1,0:T(8,128)}, f32[16]{0:T(128)S(1)}, bf16[16,384,64]{1,2,0:T(8,128)(2,1)S(1)}, /*i...) while((s32[]{:T(128)}, f32[16,384,64]{1,2,0:T(8,128)}, ...), condition=%wide.region_3.4_spmd.clone, body=%wide.region_0.3_spmd.sunk.clone | while | flops 41902472 | bytes 594653 | solution.py:61
  29.5 1.9 fusion.74
  36.7 1.9 fusion.74
  43.9 1.9 fusion.74
  51.2 1.9 fusion.74
  58.4 1.9 fusion.74
  65.6 1.9 fusion.74
  72.9 1.9 fusion.74
  80.1 1.9 fusion.74
  87.3 1.9 fusion.74
  94.5 1.9 fusion.74
  109.0 1.9 fusion.74
  116.2 1.9 fusion.74
  123.5 1.9 fusion.74
  130.7 1.9 fusion.74
  137.9 1.9 fusion.74
  142.3 28.4 %all-reduce = f32[256]{0:T(256)S(1)} all-reduce(f32[256]{0:T(256)S(1)} %dynamic-update-slice), channel_id=2, replica_groups=mesh['outer'=16,'inner'=16] {'inner'}, use_global_device_ids=true, to_apply=%add | all-reduce | flops 256 | bytes 2048
  170.8 30.4 %all-gather.10.cloned.1.call-done = f32[256,64,64]{2,1,0:T(8,128)} async-done(((f32[16,64,64]{2,1,0:T(8,128)}), f32[256,64,64]{2,1,0:T(8,128)}) %all-gather.10.cloned.1.call-update) | async-done | bytes 4194320 | tf_op jit(solution)/shard_map/all_gather | solution.py:9
  201.2 18.3 %while.48 = (s32[]{:T(128)}, f32[16]{0:T(128)S(1)}, f32[16,64,64]{2,1,0:T(8,128)S(1)}, s32[]{:T(128)}, f32[16,16]{1,0:T(8,128)S(1)}, /*index=5*/f32[16,16,64,64]{3,2,1,0:T(8,128)}) while((s32[]{:T(128)}, f32[16]{0:T(128)S(1)}, f32[16,64,64]{2,1,0:T(8,128)S(1)}, s32[]{:T(128)}, f32[16,16]{1,0:T(8,128)S(1)}, ...), condition=%wide.region_5.6_spmd.clone.clone, body=%wide.region_4.5_spmd.clone.sunk.clone | while | flops 262196 | bytes 786851 | solution.py:18
  219.5 2.0 add_select_fusion
  221.6 54.5 %all-gather.12.cloned.1.call-done = f32[256,64,64]{2,1,0:T(8,128)} async-done(((f32[16,64,64]{2,1,0:T(8,128)}), f32[256,64,64]{2,1,0:T(8,128)}) %all-gather.12.cloned.1.call-update) | async-done | bytes 4194320 | tf_op jit(solution)/shard_map/all_gather | solution.py:23
  276.1 5.2 %reduce_sum.28 = f32[16,64,64]{2,1,0:T(8,128)} reduce(f32[16,16,64,64]{3,2,1,0:T(8,128)} %bitcast.135, f32[]{:T(128)} %constant.87.clone.1), dimensions={0}, to_apply=%region_7.8 | reduce | flops 983040 | bytes 4456452 | tf_op jit(solution)/shard_map/reduce_sum | solution.py:23
  283.7 23.1 %all-reduce.1 = f32[256]{0:T(256)S(1)} all-reduce(f32[256]{0:T(256)S(1)} %fusion.37), channel_id=4, replica_groups=mesh['outer'=16,'inner'=16] {'inner'}, use_global_device_ids=true, to_apply=%add.1 | all-reduce | flops 256 | bytes 2048
  307.2 34.4 %all-reduce.2 = f32[256]{0:T(256)S(1)} all-reduce(f32[256]{0:T(256)S(1)} %dynamic-update-slice.2), channel_id=5, replica_groups=mesh['outer'=16,'inner'=16] {'outer'}, use_global_device_ids=true, to_apply=%add.2 | all-reduce | flops 256 | bytes 2048
  341.7 14.2 %all-gather.14.cloned.1.call-done = f32[256,64,64]{2,1,0:T(8,128)} async-done(((f32[16,64,64]{2,1,0:T(8,128)}), f32[256,64,64]{2,1,0:T(8,128)}) %all-gather.14.cloned.1.call-update) | async-done | bytes 4194320 | tf_op jit(solution)/shard_map/all_gather | solution.py:9
  355.9 18.2 %while.49 = (s32[]{:T(128)}, f32[16,64,64]{2,1,0:T(8,128)S(1)}, s32[]{:T(128)}, f32[16,16]{1,0:T(8,128)S(1)}, f32[16,16,64,64]{3,2,1,0:T(8,128)}) while((s32[]{:T(128)}, f32[16,64,64]{2,1,0:T(8,128)S(1)}, s32[]{:T(128)}, f32[16,16]{1,0:T(8,128)S(1)}, f32[16,16,64,64]{3,2,1,0:T(8,128)}) %tuple.107), condition=%wide.region_9.10_spmd.clone.clone, body=%wide.region_8.9_spmd.clone.sunk.clone | while | flops 262148 | bytes 786713 | solution.py:18
  374.1 2.9 multiply_reduce_fusion
  (301 shorter events, 121.9 us)
Async XLA Ops:
  6.5 1.6 copy-start
  6.5 194.6 %all-gather.10.cloned.1.call-start = ((), (), s32[]{:S(2)}) async-start(), calls=%async_computation | async-start | bytes 8912896 | tf_op jit(solution)/shard_map/all_gather | solution.py:9
  22.6 2.3 copy-start.3
  25.0 115.8 %copy-start.6 = (u32[256]{0:T(256)S(1)}, u32[256]{0:T(256)}, u32[]{:S(2)}) copy-start(u32[256]{0:T(256)} %constant.98) | copy-start | bytes 3076
  140.6 60.5 %copy-start.1 = (bf16[16,384,64]{1,2,0:T(8,128)(2,1)}, bf16[16,384,64]{1,2,0:T(8,128)(2,1)S(1)}, u32[]{:S(2)}) copy-start(bf16[16,384,64]{1,2,0:T(8,128)(2,1)S(1)} %get-tuple-element.595) | copy-start | bytes 2359300
  140.7 135.4 %all-gather.12.cloned.1.call-start = ((), (), s32[]{:S(2)}) async-start(), calls=%async_computation.1 | async-start | bytes 8912896 | tf_op jit(solution)/shard_map/all_gather | solution.py:23
  221.5 134.4 %all-gather.14.cloned.1.call-start = ((), (), s32[]{:S(2)}) async-start(), calls=%async_computation.2 | async-start | bytes 8912896 | tf_op jit(solution)/shard_map/all_gather | solution.py:9
  276.1 5.3 %copy-start.5 = (u32[256]{0:T(256)S(1)}, u32[256]{0:T(256)}, u32[]{:S(2)}) copy-start(u32[256]{0:T(256)} %constant.108) | copy-start | bytes 3076
  377.0 0.7 copy-start.4
  377.7 1.6 copy-start.2
Sparse Core Ops, SparseCore 0:
  140.8 60.3 all-gather.9
  221.6 54.3 all-gather.11
  281.4 74.4 all-gather.13
